TPU v7x, 512 devices: a whole 4x4x16 slice. The times are simulated.
512 devices in a mesh: row: 16 (over x, y_lo, core), col: 32 (over y_hi, z).
Axes of the slice: x: 4, y: 4 (y_hi: 2, y_lo: 2; y = y_hi * 2 + y_lo), z: 16, core: 2. Of those that a mesh axis runs over, the one named last changes fastest.
Arguments:
- basis_new_left: float32 [3072, 3072], P('row', 'col'), may hold values from -0.109375 to 0.109375
- basis_old_left: float32 [3072, 3072], P('row', 'col'), may hold values from -0.109375 to 0.109375
- basis_new_right: float32 [3072, 3072], P('row', 'col'), may hold values from -0.109375 to 0.109375
- basis_old_right: float32 [3072, 3072], P('row', 'col'), may hold values from -0.109375 to 0.109375
- moment: float32 [3072, 3072], P('row', 'col'), may hold values from -6 to 6
Outputs:
- rebased: float32 [3072, 3072], P('row', 'col')
All inputs are finite; a program needn't handle non-finite values.
Results may differ from a plain program's by a relative error of at most 0.000094.
Values sent between devices are 32-bit elements; how exact they have to be, the bound alone decides.
A program may use at most 64 MiB of HBM per device.

v0:
```python
import jax
import jax.numpy as jnp
from jax import lax
from jax.sharding import PartitionSpec as P


def lead_product(panel, other):
    highest = lax.Precision.HIGHEST
    return lax.dot_general(
        panel,
        other,
        (((0,), (0,)), ((), ())),
        precision=highest,
        preferred_element_type=jnp.float32,
    )


def fold_rows(piece, factor):
    highest = lax.Precision.HIGHEST
    return jnp.dot(piece, factor, precision=highest, preferred_element_type=jnp.float32)


def local(basis_new_left, basis_old_left, basis_new_right, basis_old_right, moment):
    old_panel = lax.all_gather(basis_old_right, "col", axis=1, tiled=True)
    right_block = lax.psum_scatter(
        lead_product(old_panel, basis_new_right), "row", scatter_dimension=0, tiled=True
    )
    right_columns = lax.all_gather(right_block, "row", axis=0, tiled=True)
    rotated = fold_rows(lax.all_gather(moment, "col", axis=1, tiled=True), right_columns)
    rotated_columns = lax.all_gather(rotated, "row", axis=0, tiled=True)
    fresh_panel = lax.all_gather(basis_new_left, "col", axis=1, tiled=True)
    left_block = lax.psum_scatter(
        lead_product(fresh_panel, basis_old_left), "row", scatter_dimension=0, tiled=True
    )
    return fold_rows(lax.all_gather(left_block, "col", axis=1, tiled=True), rotated_columns)


def solution(mesh):
    placed = (P("row", "col"), P("row", "col"), P("row", "col"), P("row", "col"), P("row", "col"))
    return jax.shard_map(
        local, mesh=mesh, in_specs=placed, out_specs=P("row", "col"), check_vma=False
    )
```

profile of v0, /device:TPU:1, one launch (start us, length us, event | category | flops | bytes accessed | tf_op | source)
XLA Modules:
  0.0 877.1 jit_solution(14654567181000951420)
XLA Ops:
  6.5 1.7 copy.11
  8.3 0.0 reduce-scatter.5.cloned.1.call-start
  8.3 155.4 %all-gather.11.cloned.1.call-done = f32[192,3072]{0,1:T(8,128)} async-done(((f32[192,96]{0,1:T(8,128)}), f32[192,3072]{0,1:T(8,128)}) %all-gather.11.cloned.1.call-update) | async-done | bytes 2359312 | tf_op jit(solution)/shard_map/all_gather | solution.py:24
  163.7 5.7 fusion.1
  169.4 0.0 all-gather.7.cloned.1.call-start
  169.5 0.7 copy.9
  170.2 0.0 all-gather.15.cloned.1.call-start
  170.3 0.7 copy.12
  171.0 0.0 all-gather.13.cloned.1.call-start
  171.1 70.1 %reduce-scatter.5.cloned.1.call-done = f32[192,96]{1,0:T(8,128)} async-done(((f32[3072,96]{1,0:T(8,128)}), f32[192,96]{1,0:T(8,128)}) %reduce-scatter.5.cloned.1.call-update) | async-done | bytes 73744 | tf_op jit(solution)/shard_map/reduce_scatter | solution.py:25
  241.2 0.0 reduce-scatter.7.cloned.1.call-start
  241.2 152.6 %all-gather.7.cloned.1.call-done = f32[192,3072]{0,1:T(8,128)} async-done(((f32[192,96]{0,1:T(8,128)}), f32[192,3072]{0,1:T(8,128)}) %all-gather.7.cloned.1.call-update) | async-done | bytes 2359312 | tf_op jit(solution)/shard_map/all_gather | solution.py:31
  393.9 5.7 fusion
  399.5 0.0 all-gather.17.cloned.1.call-start
  399.6 149.5 %all-gather.15.cloned.1.call-done = f32[192,3072]{0,1:T(8,128)} async-done(((f32[192,96]{0,1:T(8,128)}), f32[192,3072]{0,1:T(8,128)}) %all-gather.15.cloned.1.call-update) | async-done | bytes 2359312 | tf_op jit(solution)/shard_map/all_gather | solution.py:29
  549.1 47.4 %all-gather.13.cloned.1.call-done = f32[3072,96]{1,0:T(8,128)} async-done(((f32[192,96]{1,0:T(8,128)}), f32[3072,96]{1,0:T(8,128)}) %all-gather.13.cloned.1.call-update) | async-done | bytes 1179664 | tf_op jit(solution)/shard_map/all_gather | solution.py:28
  596.6 5.0 convolution_bitcast_fusion
  601.6 0.7 copy.13
  602.3 0.2 all-gather.9.cloned.1.call-start
  602.6 64.3 %reduce-scatter.7.cloned.1.call-done = f32[192,96]{1,0:T(8,128)} async-done(((f32[3072,96]{1,0:T(8,128)}), f32[192,96]{1,0:T(8,128)}) %reduce-scatter.7.cloned.1.call-update) | async-done | bytes 73744
  666.8 1.6 copy.16
  668.5 42.9 %all-gather.17.cloned.1.call-done = f32[3072,96]{1,0:T(8,128)} async-done(((f32[192,96]{1,0:T(8,128)}), f32[3072,96]{1,0:T(8,128)}) %all-gather.17.cloned.1.call-update) | async-done | bytes 1179664 | tf_op jit(solution)/shard_map/all_gather | solution.py:30
  711.4 150.7 %all-gather.9.cloned.1.call-done = f32[192,3072]{0,1:T(8,128)} async-done(((f32[192,96]{0,1:T(8,128)}), f32[192,3072]{0,1:T(8,128)}) %all-gather.9.cloned.1.call-update) | async-done | bytes 2359312 | tf_op jit(solution)/shard_map/all_gather | solution.py:35
  862.1 8.1 fusion.2
  (17 shorter events, 0.2 us)
Async XLA Ops:
  6.5 157.2 %copy-start = (f32[192,96]{1,0:T(8,128)S(1)}, f32[192,96]{1,0:T(8,128)}, u32[]{:S(2)}) copy-start(f32[192,96]{1,0:T(8,128)} %param.7) | copy-start | bytes 221188
  6.5 157.2 %all-gather.11.cloned.1.call-start = ((), (), s32[]{:S(2)}) async-start(), calls=%async_computation.4 | async-start | bytes 3244032 | tf_op jit(solution)/shard_map/all_gather | solution.py:24
  8.2 161.2 %copy-start.1 = (f32[192,96]{1,0:T(8,128)S(1)}, f32[192,96]{1,0:T(8,128)}, u32[]{:S(2)}) copy-start(f32[192,96]{1,0:T(8,128)} %param.5) | copy-start | bytes 221188
  8.2 162.0 %copy-start.2 = (f32[192,96]{1,0:T(8,128)S(1)}, f32[192,96]{1,0:T(8,128)}, u32[]{:S(2)}) copy-start(f32[192,96]{1,0:T(8,128)} %param.9) | copy-start | bytes 221188
  8.2 385.6 %copy-start.3 = (f32[192,96]{1,0:T(8,128)S(1)}, f32[192,96]{1,0:T(8,128)}, u32[]{:S(2)}) copy-start(f32[192,96]{1,0:T(8,128)} %param.6) | copy-start | bytes 221188
  8.3 232.9 %reduce-scatter.5.cloned.1.call-start = ((), (), s32[]{:S(2)}) async-start(), calls=%async_computation.5 | async-start | bytes 1671168 | tf_op jit(solution)/shard_map/reduce_scatter | solution.py:25
  169.4 224.5 %all-gather.7.cloned.1.call-start = ((), (), s32[]{:S(2)}) async-start(), calls=%async_computation.2 | async-start | bytes 3244032 | tf_op jit(solution)/shard_map/all_gather | solution.py:31
  170.2 378.9 %all-gather.15.cloned.1.call-start = ((), (), s32[]{:S(2)}) async-start(), calls=%async_computation.7 | async-start | bytes 3244032 | tf_op jit(solution)/shard_map/all_gather | solution.py:29
  171.0 425.5 %all-gather.13.cloned.1.call-start = ((), (), s32[]{:S(2)}) async-start(), calls=%async_computation.6 | async-start | bytes 1671168 | tf_op jit(solution)/shard_map/all_gather | solution.py:28
  241.2 425.7 %reduce-scatter.7.cloned.1.call-start = ((), (), s32[]{:S(2)}) async-start(), calls=%async_computation.9 | async-start | bytes 1671168
  399.5 311.9 %all-gather.17.cloned.1.call-start = ((), (), s32[]{:S(2)}) async-start(), calls=%async_computation.8 | async-start | bytes 1671168 | tf_op jit(solution)/shard_map/all_gather | solution.py:30
  602.3 259.8 %all-gather.9.cloned.1.call-start = ((), (), s32[]{:S(2)}) async-start(), calls=%async_computation.3 | async-start | bytes 3244032 | tf_op jit(solution)/shard_map/all_gather | solution.py:35
Sparse Core Ops, SparseCore 0:
  10.5 153.2 all-gather.10
  169.5 71.5 reduce-scatter.4
  244.7 149.0 all-gather.6
  397.3 151.7 all-gather.14
  551.3 45.1 all-gather.12
  599.5 67.3 reduce-scatter.6
  669.0 42.3 all-gather.16
  714.5 147.5 all-gather.8
where the time goes:
time: 886 us; the launch traced here: 877 us
  waiting for transfers between devices  833 us (94%)
  matrix products  24.5 us (3%)
  between operations  13.6 us (2%)
    all_gather x1, waiting for transfers between devices, local(): old_panel = lax.all_gather(basis_old_right, 'col', axis=1, tiled=True)  155 us
    all_gather x1, waiting for transfers between devices, local(): fresh_panel = lax.all_gather(basis_new_left, 'col', axis=1, tiled=True)  153 us
    all_gather x1, waiting for transfers between devices, local(): lax.all_gather(left_block, 'col', axis=1, tiled=True)  151 us
    all_gather x1, waiting for transfers between devices, local(): lax.all_gather(moment, 'col', axis=1, tiled=True)  150 us
    reduce_scatter x1, waiting for transfers between devices, local(): lax.psum_scatter(lead_product(old_panel, basis_new_right), 'row', scatter...  70.1 us
    unnamed x9, waiting for transfers between devices  64.4 us
    all_gather x1, waiting for transfers between devices, local(): right_columns = lax.all_gather(right_block, 'row', axis=0, tiled=True)  47.4 us
    all_gather x1, waiting for transfers between devices, local(): rotated_columns = lax.all_gather(rotated, 'row', axis=0, tiled=True)  42.9 us
  transfers between devices with their start and end apart: 8, of which 8 were waited for; matrix products, arithmetic and copies ran while one was open for 2% of the time, Pallas kernels for 0%

commit v1 on v0

v1 whole, which is shorter than its diff:
```python
import functools

import jax
import jax.numpy as jnp
from jax import lax
from jax.experimental import pallas as pl
from jax.experimental.pallas import tpu as pltpu
from jax.sharding import PartitionSpec as P

MESH = pl.DeviceIdType.MESH
F32, BF16 = jnp.float32, jnp.bfloat16
OLD_R, MOM, OLD_L, NEW_L = 0, 1, 2, 3
NCH = 2
OFFSETS = (0.0, 0.2, 6.0, 6.2)
NN = (((1,), (0,)), ((), ()))
NT = (((1,), (1,)), ((), ()))


def split(value):
    high = value.astype(BF16)
    return high, (value - high.astype(F32)).astype(BF16)


def dot3(a, b, dims):
    def one(u, v):
        return lax.dot_general(u, v, dims, preferred_element_type=F32)

    return one(a[0], b[0]) + (one(a[0], b[1]) + one(a[1], b[0]))


def kernel(c_ref, m_ref, b_ref, a_ref, d_ref, o_ref, *scratch):
    (pk, rb, dsend, drecv, dth, dtl, tmp, rp, rsib, rsum, rrs, rg, mh, ml, bh, bl, ah, al,
     tp, trecv, tfin, tg, th, tl, up, urecv, vp, vsib, vsum, vrecv,
     ring_s, ring_r, d_s, d_r, g2_s, g2_r, g3_s, g3_r, g5_s, g5_r, g6_s, g6_r,
     te_s, te_r, tm_s, tm_r, tf_s, tf_r, ue_s, ue_r, vs_s, vs_r, vr_s, vr_r) = scratch
    r, q = lax.axis_index("row"), lax.axis_index("col")
    p, c = r // 2, lax.rem(r, 2)
    h, z = q // 16, lax.rem(q, 16)
    sibling = (p * 2 + (1 - c), q)
    partner = (r, (1 - h) * 16 + z)
    ring_to = ((r, h * 16 + lax.rem(z + 1, 16)), (r, h * 16 + lax.rem(z + 15, 16)))

    def chip(k, plane):
        return (lax.rem(p + k, 8) * 2 + c, plane * 16 + z)

    barrier = pltpu.get_barrier_semaphore()
    greeted = [sibling, ring_to[0], ring_to[1], partner]
    greeted += [chip(k, plane) for k in range(1, 8) for plane in (h, 1 - h)]
    for device in greeted:
        pl.semaphore_signal(barrier, inc=1, device_id=device, device_id_type=MESH)

    own = (c_ref, m_ref, b_ref, a_ref)
    for index, ref in enumerate(own):
        pk[index, :, 0:96] = ref[0:144, :]
        for part in range(3):
            pk[index, 48 * part:48 * part + 48, 96:128] = ref[144:192, 32 * part:32 * part + 32]
    dsend[:, 0:96] = d_ref[...]
    dsend[:, 96:128] = jnp.zeros((192, 32), F32)
    pl.semaphore_wait(barrier, len(greeted))

    def remote(src, dst, send, recv, device):
        return pltpu.make_async_remote_copy(
            src_ref=src, dst_ref=dst, send_sem=send, recv_sem=recv, device_id=device, device_id_type=MESH
        )

    finish = []

    def go(copy):
        copy.start()
        finish.append(copy)
        return copy

    def ring(m, d, s, ch):
        if s == 8:
            rows, dst = pl.ds(72 * d, 72), rb.at[m, 0, 7]
        else:
            rows, dst = pl.ds(ch * (144 // NCH), 144 // NCH), rb.at[m, d, s - 1]
        src = pk.at[m] if s == 1 else rb.at[m, d, s - 2]
        return remote(src.at[rows], dst.at[rows], ring_s.at[m, d, s - 1, ch], ring_r.at[m, d, s - 1, ch], ring_to[d])

    waited = set()

    def arrived(m, d, s, ch):
        if s >= 1 and (m, d, s, ch) not in waited:
            waited.add((m, d, s, ch))
            ring(m, d, s, ch).wait_recv()

    def send_step(m, s):
        for ch in range(NCH if s < 8 else 1):
            for d in range(2):
                for before in ([ch] if s < 8 else range(NCH)):
                    arrived(m, d, s - 1, before)
                go(ring(m, d, s, ch))

    def unpacked(src):
        lane = lax.broadcasted_iota(jnp.int32, (144, 128), 1)
        tmp[0:144, :] = jnp.where(lane < 96, src[...], 0.0)
        for part in range(3):
            tmp[144:192, 32 * part:32 * part + 32] = src[48 * part:48 * part + 48, 96:128]
        return split(tmp[...])

    def store(m, d, e, value):
        high, low = value
        if m == OLD_R:
            lanes = slice(128 * (e % 4), 128 * (e % 4) + 128)
            rp[d, e // 4, :, lanes] = dot3((dth[...], dtl[...]), value, NN)
        elif m == MOM:
            mh[d, :, 128 * e:128 * e + 128] = high
            ml[d, :, 128 * e:128 * e + 128] = low
        else:
            origin = lax.rem(z + (16 - (e + 1) if d == 0 else e), 16)
            lanes = pl.ds(pl.multiple_of(origin * 128, 128), 128)
            hs, ls = (bh, bl) if m == OLD_L else (ah, al)
            hs[:, lanes] = high
            ls[:, lanes] = low

    def own_block(m):
        tmp[:, 0:96] = own[m][...]
        store(m, 1, 0, split(tmp[...]))

    def take(m, s):
        for d in range(2):
            if s == 8:
                arrived(m, d, 8, 0)
            else:
                for ch in range(NCH):
                    arrived(m, d, s, ch)
        store(m, 0, s - 1, unpacked(rb.at[m, 0, s - 1]))
        if s < 8:
            store(m, 1, s, unpacked(rb.at[m, 1, s - 1]))

    def rows_of(index):
        return pl.ds(pl.multiple_of(index * 24, 8), 24)

    def r_sibling(g):
        go(remote(rp.at[1 - c, g], rsib.at[g], g2_s.at[g], g2_r.at[g], sibling))

    def r_scatter(g):
        remote(rp.at[1 - c, g], rsib.at[g], g2_s.at[g], g2_r.at[g], sibling).wait_recv()
        rsum[g] = rp[c, g] + rsib[g]
        for k in range(1, 8):
            go(r_piece(g, k))

    def r_piece(g, k):
        target = lax.rem(p + k, 8)
        return remote(rsum.at[g, rows_of(target)], rrs.at[g, k - 1], g3_s.at[g, k - 1], g3_r.at[g, k - 1], chip(k, h))

    def r_whole(g, k):
        mine = rg.at[c, g, rows_of(p)]
        return remote(mine, mine, g5_s.at[g, k - 1], g5_r.at[g, k - 1], chip(k, h))

    def r_gather(g):
        total = rsum[g, rows_of(p), :]
        for k in range(1, 8):
            r_piece(g, k).wait_recv()
            total = total + rrs[g, k - 1]
        rg[c, g, rows_of(p), :] = total
        for k in range(1, 8):
            go(r_whole(g, k))

    def r_forward(g):
        for k in range(1, 8):
            r_whole(g, k).wait_recv()
        go(remote(rg.at[c, g], rg.at[c, g], g6_s.at[g], g6_r.at[g], sibling))

    def t_partial():
        for g in range(2):
            remote(rg.at[c, g], rg.at[c, g], g6_s.at[g], g6_r.at[g], sibling).wait_recv()
        for half in range(2):
            total = None
            for d in range(2):
                for g in range(2):
                    lanes = slice(512 * g, 512 * g + 512)
                    rows = slice(96 * half, 96 * half + 96)
                    term = dot3(split(rg[d, g]), (mh[d, rows, lanes], ml[d, rows, lanes]), NT)
                    total = term if total is None else total + term
            tp[:, 128 * half:128 * half + 96] = total
            tp[:, 128 * half + 96:128 * half + 128] = jnp.zeros((192, 32), F32)
        go(t_exchange())

    def half_of(plane):
        return pl.ds(pl.multiple_of(plane * 96, 8), 96)

    def t_exchange():
        return remote(tp.at[half_of(1 - h)], trecv, te_s.at[0], te_r.at[0], partner)

    plane_of = r // 8

    def t_piece(k):
        return remote(tfin, tg.at[c, lax.rem(p, 4), h], tm_s.at[k], tm_r.at[lax.rem(p, 4), h], chip(k, plane_of))

    def t_spread():
        t_exchange().wait_recv()
        tfin[...] = tp[half_of(h), :] + trecv[...]
        for k in range(1, 8):
            go(t_piece(k))

        @pl.when(plane_of != h)
        def _():
            t_piece(0).start()

        @pl.when(plane_of == h)
        def _():
            pltpu.make_async_copy(tfin, tg.at[c, lax.rem(p, 4), h], tm_r.at[lax.rem(p, 4), h]).start()

    def t_forward():
        for j in range(4):
            for plane in range(2):
                pltpu.make_async_copy(tfin, tg.at[c, j, plane], tm_r.at[j, plane]).wait()
        go(remote(tg.at[c], tg.at[c], tf_s.at[0], tf_r.at[0], sibling))

    def u_partial():
        remote(tg.at[c], tg.at[c], tf_s.at[0], tf_r.at[0], sibling).wait_recv()
        for core in range(2):
            for j in range(4):
                for plane in range(2):
                    high, low = split(tg[core, j, plane])
                    lanes = slice(256 * (2 * j + core), 256 * (2 * j + core) + 256)
                    th[96 * plane:96 * plane + 96, lanes] = high
                    tl[96 * plane:96 * plane + 96, lanes] = low
        up[:, 0:192] = dot3((th[...], tl[...]), (bh[...], bl[...]), NT)
        up[:, 192:256] = jnp.zeros((192, 64), F32)
        go(remote(up, urecv, ue_s.at[0], ue_r.at[0], partner))

    def v_sibling(k):
        return remote(vp.at[1 - c, k], vsib.at[k], vs_s.at[k], vs_r.at[k], sibling)

    def v_partial():
        remote(up, urecv, ue_s.at[0], ue_r.at[0], partner).wait_recv()
        whole = split(up[:, 0:192] + urecv[:, 0:192])
        for k in range(4):
            for core in range(2):
                lanes = slice(256 * (2 * k + core), 256 * (2 * k + core) + 256)
                vp[core, k] = dot3(whole, (ah[:, lanes], al[:, lanes]), NN)
            go(v_sibling(k))

    def v_piece(k, plane):
        target = lax.rem(p + k, 4)
        return remote(
            vsum.at[target, pl.ds(96 * plane, 96)], vrecv.at[p], vr_s.at[k, plane], vr_r.at[p],
            ((4 * h + target) * 2 + c, plane * 16 + z),
        )

    def v_scatter():
        for k in range(4):
            v_sibling(k).wait_recv()
            vsum[k] = vp[c, k] + vsib[k]
        for k in range(4):
            for plane in range(2):
                target = lax.rem(p + k, 4)
                here = jnp.logical_and(4 * h + target == p, h == plane)

                @pl.when(jnp.logical_not(here))
                def _():
                    v_piece(k, plane).start()

                @pl.when(here)
                def _():
                    pltpu.make_async_copy(vsum.at[target, pl.ds(96 * plane, 96)], vrecv.at[p], vr_r.at[p]).start()

    def v_result():
        total = None
        for k in range(8):
            pltpu.make_async_copy(vsum.at[0, pl.ds(0, 96)], vrecv.at[k], vr_r.at[k]).wait()
            total = vrecv[k] if total is None else total + vrecv[k]
        turned = total.T
        o_ref[0:96, :] = turned[0:96, :]
        o_ref[96:192, :] = turned[128:224, :]

    events = sorted((OFFSETS[m] + s, m, s) for m in range(4) for s in range(1, 10))
    hooks = {
        (OLD_R, 6): [lambda: r_sibling(0)],
        (OLD_R, 7): [lambda: r_scatter(0)],
        (OLD_R, 9): [lambda: r_sibling(1)],
        (MOM, 9): [lambda: r_gather(0)],
        (OLD_L, 3): [lambda: r_scatter(1)],
        (OLD_L, 4): [lambda: r_gather(1)],
        (NEW_L, 4): [lambda: r_forward(0)],
        (OLD_L, 5): [lambda: r_forward(1)],
        (NEW_L, 5): [t_partial],
        (NEW_L, 6): [t_spread],
        (NEW_L, 7): [t_forward],
        (OLD_L, 9): [u_partial],
        (NEW_L, 9): [v_partial, v_scatter, v_result],
    }
    tmp[:, 96:128] = jnp.zeros((192, 32), F32)
    d_copy = remote(dsend, drecv, d_s.at[0], d_r.at[0], partner)
    for _, m, s in events:
        if s <= 8:
            send_step(m, s)
        if s == 1:
            if m == OLD_R:
                go(d_copy)
        if s == 2 and m == OLD_R:
            d_copy.wait_recv()
            for ref, plane in ((dsend, h), (drecv, 1 - h)):
                high, low = split(ref[...].T[0:96, :])
                dth[pl.ds(pl.multiple_of(plane * 96, 16), 96), :] = high
                dtl[pl.ds(pl.multiple_of(plane * 96, 16), 96), :] = low
            own_block(OLD_R)
        elif s == 1 and m != OLD_R:
            own_block(m)
        if s >= 2:
            take(m, s - 1)
        for hook in hooks.get((m, s), []):
            hook()

    for copy in finish:
        copy.wait_send()

    @pl.when(plane_of != h)
    def _():
        t_piece(0).wait_send()

    for k in range(4):
        for plane in range(2):
            here = jnp.logical_and(4 * h + lax.rem(p + k, 4) == p, h == plane)

            @pl.when(jnp.logical_not(here))
            def _():
                v_piece(k, plane).wait_send()


def local(basis_new_left, basis_old_left, basis_new_right, basis_old_right, moment):
    vmem, dma = pltpu.VMEM, pltpu.SemaphoreType.DMA
    scratch = [
        vmem((4, 144, 128), F32), vmem((4, 2, 8, 144, 128), F32),
        vmem((192, 128), F32), vmem((192, 128), F32), vmem((192, 192), BF16), vmem((192, 192), BF16),
        vmem((192, 128), F32),
        vmem((2, 2, 192, 512), F32), vmem((2, 192, 512), F32), vmem((2, 192, 512), F32),
        vmem((2, 7, 24, 512), F32), vmem((2, 2, 192, 512), F32),
        vmem((2, 192, 1024), BF16), vmem((2, 192, 1024), BF16),
        vmem((192, 2048), BF16), vmem((192, 2048), BF16), vmem((192, 2048), BF16), vmem((192, 2048), BF16),
        vmem((192, 256), F32), vmem((96, 256), F32), vmem((96, 256), F32), vmem((2, 4, 2, 96, 256), F32),
        vmem((192, 2048), BF16), vmem((192, 2048), BF16),
        vmem((192, 256), F32), vmem((192, 256), F32),
        vmem((2, 4, 192, 256), F32), vmem((4, 192, 256), F32), vmem((4, 192, 256), F32), vmem((8, 96, 256), F32),
        dma((4, 2, 8, NCH)), dma((4, 2, 8, NCH)), dma((1,)), dma((1,)),
        dma((2,)), dma((2,)), dma((2, 7)), dma((2, 7)), dma((2, 7)), dma((2, 7)), dma((2,)), dma((2,)),
        dma((1,)), dma((1,)), dma((8,)), dma((4, 2)), dma((1,)), dma((1,)), dma((1,)), dma((1,)),
        dma((4,)), dma((4,)), dma((4, 2)), dma((8,)),
    ]
    return pl.pallas_call(
        kernel,
        out_shape=jax.ShapeDtypeStruct((192, 96), F32),
        in_specs=[pl.BlockSpec(memory_space=pltpu.VMEM)] * 5,
        out_specs=pl.BlockSpec(memory_space=pltpu.VMEM),
        scratch_shapes=scratch,
        compiler_params=pltpu.CompilerParams(
            collective_id=0, has_side_effects=True, vmem_limit_bytes=48 << 20
        ),
    )(basis_old_right, moment, basis_old_left, basis_new_left, basis_new_right)


def solution(mesh):
    placed = (P("row", "col"),) * 5
    return jax.shard_map(local, mesh=mesh, in_specs=placed, out_specs=P("row", "col"), check_vma=False)
```

time: 886 us -> 129 us (0.15)
  waiting for transfers between devices: 833 us -> 0 us
  Pallas kernels: 0 us -> 122 us
  matrix products: 24.5 us -> 0 us
  between operations: 13.6 us -> 0.01 us
    all_gather x6 -> x0, waiting for transfers between devices: 699 us -> none  [the longest x1 155 us: local(): old_panel = lax.all_gather(basis_old_right, 'col', axis=1, tiled=True)]
    pallas_call x0 -> x1, Pallas kernels: none -> 122 us  [local(): pl.pallas_call(kernel, out_shape=jax.ShapeDtypeStruct((192, 96), F32), in...]
    reduce_scatter x1 -> x0, waiting for transfers between devices: 70.1 us -> none  [local(): lax.psum_scatter(lead_product(old_panel, basis_new_right), 'row', scatter...]
    unnamed x9 -> x0, waiting for transfers between devices: 64.4 us -> none
    dot_general x3 -> x0, matrix products: 18.8 us -> none  [the longest x2 13.2 us: fold_rows(): jnp.dot(piece, factor, precision=highest, preferred_element_type=jnp.floa...]
  transfers between devices with their start and end apart: 8 -> 0, of which waited for: 8 -> 0; matrix products, arithmetic and copies ran while one was open for 2% -> 0% of each run, Pallas kernels for 0% -> 0%
where the time goes in v1:
time: 129 us; the launch traced here: 127 us
  Pallas kernels  122 us (95%)
  local copies, waits for them, and re-layouts  5.1 us (4%)
    pallas_call x1, Pallas kernels, local(): pl.pallas_call(kernel, out_shape=jax.ShapeDtypeStruct((192, 96), F32), in...  122 us
    unnamed x11, local copies, waits for them, and re-layouts  5.1 us

profile of v1, /device:TPU:1, one launch (start us, length us, event | category | flops | bytes accessed | tf_op | source)
XLA Modules:
  0.0 126.9 jit_solution(2122156357269771067)
XLA Ops:
  0.0 0.0 copy-start
  0.0 0.9 copy-done
  0.9 0.0 copy-start.1
  0.9 0.9 copy-done.1
  1.8 0.0 copy-start.2
  1.8 0.9 copy-done.2
  2.7 0.0 copy-start.3
  2.7 0.9 copy-done.3
  3.6 0.0 copy-start.4
  3.6 0.9 copy-done.4
  4.5 121.8 %shard_map.55 = f32[192,96]{1,0:T(8,128)S(1)} custom-call(f32[192,96]{1,0:T(8,128)S(1)} %copy-done, f32[192,96]{1,0:T(8,128)S(1)} %copy-done.1, f32[192,96]{1,0:T(8,128)S(1)} %copy-done.2, f32[192,96]{1,0:T(8,128)S(1)} %copy-done.3, f32[192,96]{1,0:T(8,128)S(1)} %copy-done.4), custom_call_target="tpu_custom_call" | custom-call | tf_op jit(solution)/shard_map/pallas_call | solution.py:343
  126.2 0.6 copy.7
Async XLA Ops:
  0.0 0.9 copy-start
  0.9 0.9 copy-start.1
  1.8 0.9 copy-start.2
  2.7 0.9 copy-start.3
  3.6 0.9 copy-start.4

commit v2 on v1

v2 whole, which is shorter than its diff:
```python
import functools

import jax
import jax.numpy as jnp
from jax import lax
from jax.experimental import pallas as pl
from jax.experimental.pallas import tpu as pltpu
from jax.sharding import PartitionSpec as P

MESH = pl.DeviceIdType.MESH
F32, BF16 = jnp.float32, jnp.bfloat16
OLD_R, MOM, OLD_L, NEW_L = 0, 1, 2, 3
NCH = 2
STARTS = (0.0, 0.5, 13.0, 13.5)
RATES = (4.0, 3.6, 4.4, 4.4)
EVENTS = [(STARTS[0] + RATES[0] * s, "fast", OLD_R, s) for s in range(5)]
EVENTS += [(STARTS[m] + RATES[m] * (s - 1), "ring", m, s) for m in (MOM, OLD_L, NEW_L) for s in range(1, 10)]
EVENTS += [
    (0.1, "spread_d", None, 0), (0.2, "load_m", None, 0), (0.8, "swap_start", OLD_L, 0), (0.9, "swap_start", NEW_L, 0),
    (3.0, "turn_d", None, 0), (12.8, "swap_end", OLD_L, 0), (12.9, "swap_end", NEW_L, 0),
    (8.1, "r_sibling", 0, 0), (10.0, "r_scatter", 0, 0), (14.0, "r_gather", 0, 0), (18.5, "r_forward", 0, 0),
    (16.1, "r_sibling", 1, 0), (17.8, "r_scatter", 1, 0), (22.5, "r_gather", 1, 0), (27.0, "r_forward", 1, 0),
    (29.5, "t_partial", None, 0), (33.0, "t_spread", None, 0),
    (38.0, "t_forward", None, 0), (48.3, "u_partial", None, 0),
    (49.0, "v_partial", None, 0), (49.1, "v_scatter", None, 0), (49.2, "v_result", None, 0),
]
NN = (((1,), (0,)), ((), ()))
NT = (((1,), (1,)), ((), ()))


def split(value):
    high = value.astype(BF16)
    return high, (value - high.astype(F32)).astype(BF16)


def dot3(a, b, dims):
    def one(u, v):
        return lax.dot_general(u, v, dims, preferred_element_type=F32)

    return one(a[0], b[0]) + (one(a[0], b[1]) + one(a[1], b[0]))


def kernel(c_ref, m_ref, b_ref, a_ref, d_ref, o_ref, *scratch):
    (inp, sw, wide, turned, pk, rb, dsend, drecv, dth, dtl, tmp, rp, rsib, rsum, rrs, rg, mh, ml, bh, bl, ah, al,
     tp, trecv, tfin, tg, th, tl, up, urecv, vp, vsib, vsum, vrecv,
     in_s, sw_s, sw_r, ring_s, ring_r, d_s, d_r, g2_s, g2_r, g3_s, g3_r, g5_s, g5_r, g6_s, g6_r,
     te_s, te_r, tm_s, tm_r, tf_s, tf_r, ue_s, ue_r, vs_s, vs_r, vr_s, vr_r) = scratch
    r, q = lax.axis_index("row"), lax.axis_index("col")
    p, c = r // 2, lax.rem(r, 2)
    h, z = q // 16, lax.rem(q, 16)
    half, place = p // 4, lax.rem(p, 4)
    sibling = (p * 2 + (1 - c), q)
    partner = (r, (1 - h) * 16 + z)
    ring_to = tuple((r, h * 16 + lax.rem(z + k, 16)) for k in (1, 15, 2, 14))

    def chip(k):
        return (lax.rem(p + k, 8) * 2 + c, q)

    def near(k, other):
        return ((4 * half + lax.rem(place + k, 4)) * 2 + c, ((1 - h) if other else h) * 16 + z)

    across = ((4 * (1 - half) + place) * 2 + c, (1 - h) * 16 + z)

    barrier = pltpu.get_barrier_semaphore()
    greeted = [sibling, across, *ring_to]
    greeted += [chip(k) for k in range(1, 8)] + [near(k, True) for k in range(4)]
    for device in greeted:
        pl.semaphore_signal(barrier, inc=1, device_id=device, device_id_type=MESH)

    loads = [pltpu.make_async_copy(ref, inp.at[i], in_s.at[i]) for i, ref in enumerate((c_ref, d_ref, m_ref, b_ref, a_ref))]
    for load in loads:
        load.start()

    def pack(source, dst):
        dst[:, 0:96] = source[0:144, :]
        for part in range(3):
            dst[48 * part:48 * part + 48, 96:128] = source[144:192, 32 * part:32 * part + 32]

    loads[0].wait()
    pack(inp.at[0], pk.at[OLD_R])
    pl.semaphore_wait(barrier, len(greeted))

    def remote(src, dst, send, recv, device):
        return pltpu.make_async_remote_copy(
            src_ref=src, dst_ref=dst, send_sem=send, recv_sem=recv, device_id=device, device_id_type=MESH
        )

    finish = []

    def go(copy):
        copy.start()
        finish.append(copy)
        return copy

    def ring(m, d, s, ch):
        if s == 8:
            rows, dst = pl.ds(72 * d, 72), rb.at[m, 0, 7]
        else:
            rows, dst = pl.ds(ch * (144 // NCH), 144 // NCH), rb.at[m, d, s - 1]
        back = 2 if m == OLD_R and s % 2 == 0 else 1
        src = pk.at[m] if s == back else rb.at[m, d, s - back - 1]
        return remote(
            src.at[rows], dst.at[rows], ring_s.at[m, d, s - 1, ch], ring_r.at[m, d, s - 1, ch],
            ring_to[d + 2 * (back - 1)],
        )

    waited = set()

    def arrived(m, d, s, ch):
        if s >= 1 and (m, d, s, ch) not in waited:
            waited.add((m, d, s, ch))
            ring(m, d, s, ch).wait_recv()

    def send_step(m, s):
        for ch in range(NCH if s < 8 else 1):
            for d in range(2):
                for before in ([ch] if s < 8 else range(NCH)):
                    arrived(m, d, s - 1, before)
                go(ring(m, d, s, ch))

    def fast_step(s):
        for ch in range(NCH):
            if s > 0:
                for d in range(2):
                    arrived(OLD_R, d, 2 * s, ch)
            if s < 3:
                for d in range(2):
                    go(ring(OLD_R, d, 2 * s + 2, ch))
            elif ch == NCH - 1:
                for d in range(2):
                    go(ring(OLD_R, d, 8, 0))
            for d in range(2):
                go(ring(OLD_R, d, 2 * s + 1, ch))

    def unpacked(src):
        lane = lax.broadcasted_iota(jnp.int32, (144, 128), 1)
        tmp[0:144, :] = jnp.where(lane < 96, src[...], 0.0)
        for part in range(3):
            tmp[144:192, 32 * part:32 * part + 32] = src[48 * part:48 * part + 48, 96:128]
        return split(tmp[...])

    def store(m, d, e, value):
        high, low = value
        if m == OLD_R:
            rp[d, :, 96 * e:96 * e + 96] = dot3((dth[...], dtl[...]), value, NN)[:, 0:96]
        elif m == MOM:
            mh[d, :, 96 * e:96 * e + 96] = high[:, 0:96]
            ml[d, :, 96 * e:96 * e + 96] = low[:, 0:96]
        else:
            origin = lax.rem(z + (16 - (e + 1) if d == 0 else e), 16)
            lanes = pl.ds(pl.multiple_of(origin * 128, 128), 128)
            hs, ls = (bh, bl) if m == OLD_L else (ah, al)
            hs[:, lanes] = high
            ls[:, lanes] = low

    def own_block(m):
        if m == OLD_R or m == MOM:
            tmp[:, 0:96] = inp[0 if m == OLD_R else 2]
            store(m, 1, 0, split(tmp[...]))
        else:
            store(m, 1, 0, unpacked(pk.at[m]))

    def swap(m):
        return remote(sw.at[m - 2], pk.at[m], sw_s.at[m - 2], sw_r.at[m - 2], across)

    def swap_start(m):
        loads[m + 1].wait()
        pack(inp.at[m + 1], sw.at[m - 2])

        @pl.when(half != h)
        def _():
            swap(m).start()

        @pl.when(half == h)
        def _():
            pltpu.make_async_copy(sw.at[m - 2], pk.at[m], sw_r.at[m - 2]).start()

    def swap_end(m):
        pltpu.make_async_copy(sw.at[m - 2], pk.at[m], sw_r.at[m - 2]).wait()

    def take(m, s):
        for d in range(2):
            if s == 8:
                arrived(m, d, 8, 0)
            else:
                for ch in range(NCH):
                    arrived(m, d, s, ch)
        store(m, 0, s - 1, unpacked(rb.at[m, 0, s - 1]))
        if s < 8:
            store(m, 1, s, unpacked(rb.at[m, 1, s - 1]))

    def rows_of(index):
        return pl.ds(pl.multiple_of(index * 24, 8), 24)

    def lanes_of(g):
        return pl.ds(384 * g, 384)

    def r_pair(g):
        return remote(rp.at[1 - c, :, lanes_of(g)], rsib.at[:, lanes_of(g)], g2_s.at[g], g2_r.at[g], sibling)

    def r_sibling(g):
        go(r_pair(g))

    def r_scatter(g):
        r_pair(g).wait_recv()
        rsum[:, lanes_of(g)] = rp[c, :, lanes_of(g)] + rsib[:, lanes_of(g)]
        for k in range(1, 8):
            go(r_piece(g, k))

    def r_piece(g, k):
        src = rsum.at[rows_of(lax.rem(p + k, 8)), lanes_of(g)]
        return remote(src, rrs.at[k - 1, :, lanes_of(g)], g3_s.at[g, k - 1], g3_r.at[g, k - 1], chip(k))

    def r_whole(g, k):
        mine = rg.at[c, rows_of(p), lanes_of(g)]
        return remote(mine, mine, g5_s.at[g, k - 1], g5_r.at[g, k - 1], chip(k))

    def r_gather(g):
        total = rsum[rows_of(p), lanes_of(g)]
        for k in range(1, 8):
            r_piece(g, k).wait_recv()
            total = total + rrs[k - 1, :, lanes_of(g)]
        rg[c, rows_of(p), lanes_of(g)] = total
        for k in range(1, 8):
            go(r_whole(g, k))

    def r_last(g):
        both = rg.at[c, :, lanes_of(g)]
        return remote(both, both, g6_s.at[g], g6_r.at[g], sibling)

    def r_forward(g):
        for k in range(1, 8):
            r_whole(g, k).wait_recv()
        go(r_last(g))

    def t_partial():
        for g in range(2):
            r_last(g).wait_recv()
        factor = (split(rg[0]), split(rg[1]))
        parts = []
        for part in range(2):
            rows = slice(96 * part, 96 * part + 96)
            total = dot3(factor[0], (mh[0, rows, :], ml[0, rows, :]), NT)
            parts.append(total + dot3(factor[1], (mh[1, rows, :], ml[1, rows, :]), NT))
        for side in range(2):
            rows = slice(96 * side, 96 * side + 96)
            fold(tp.at[side], parts[0][rows, :], parts[1][rows, :])
        go(t_exchange())

    def fold(dst, first, second):
        dst[0:96, 0:96] = first
        dst[0:96, 96:128] = second[:, 0:32]
        dst[96:144, 0:64] = second[0:48, 32:96]
        dst[96:144, 64:128] = second[48:96, 32:96]

    def unfold(value):
        wide[:, 0:96] = value[0:96, 0:96]
        wide[:, 128:160] = value[0:96, 96:128]
        wide[0:48, 160:224] = value[96:144, 0:64]
        wide[48:96, 160:224] = value[96:144, 64:128]
        return wide[...]

    def t_exchange():
        return remote(tp.at[1 - h], trecv, te_s.at[0], te_r.at[0], partner)

    def t_piece(k, other):
        return remote(tfin, tg.at[c, place, h], tm_s.at[k, other], tm_r.at[k, other], near(k, other))

    def t_spread():
        t_exchange().wait_recv()
        total = tp[h] + trecv[...]
        tfin[...] = total
        tg[c, place, h] = total
        for k in range(4):
            for other in range(2):
                if k or other:
                    go(t_piece(k, other))

    def t_last():
        return remote(tg.at[c], tg.at[c], tf_s.at[0], tf_r.at[0], sibling)

    def t_forward():
        for k in range(4):
            for other in range(2):
                if k or other:
                    t_piece(k, other).wait_recv()
        go(t_last())

    def u_exchange():
        return remote(up, urecv, ue_s.at[0], ue_r.at[0], chip(4))

    def u_partial():
        t_last().wait_recv()
        for core in range(2):
            for j in range(4):
                for plane in range(2):
                    high, low = split(unfold(tg[core, j, plane]))
                    lanes = slice(256 * (2 * j + core), 256 * (2 * j + core) + 256)
                    th[96 * plane:96 * plane + 96, lanes] = high
                    tl[96 * plane:96 * plane + 96, lanes] = low
        total = dot3((th[...], tl[...]), (bh[...], bl[...]), NT)
        up[0:192, :] = total[:, 0:128]
        up[192:288, 0:64] = total[0:96, 128:192]
        up[192:288, 64:128] = total[96:192, 128:192]
        go(u_exchange())

    def v_sibling(k):
        target = lax.rem(place + k, 4)
        return remote(vp.at[1 - c, target], vsib.at[target], vs_s.at[k], vs_r.at[k], sibling)

    def v_partial():
        u_exchange().wait_recv()
        total = up[...] + urecv[...]
        turned[:, 0:128] = total[0:192, :]
        turned[0:96, 128:192] = total[192:288, 0:64]
        turned[96:192, 128:192] = total[192:288, 64:128]
        whole = split(turned[...])
        for k in range(4):
            target = lax.rem(place + k, 4)
            for core in range(2):
                lanes = pl.ds(pl.multiple_of(256 * (2 * target + core), 256), 256)
                term = dot3(whole, (ah[:, lanes], al[:, lanes]), NN)
                for side in range(2):
                    rows = slice(96 * side, 96 * side + 96)
                    fold(vp.at[core, target, side], term[rows, 0:96], term[rows, 128:224])
            go(v_sibling(k))

    def v_piece(k, other):
        src = vsum.at[lax.rem(place + k, 4), (1 - h) if other else h]
        return remote(src, vrecv.at[k, other], vr_s.at[k, other], vr_r.at[k, other], near(k, other))

    def v_scatter():
        for k in range(4):
            v_sibling(k).wait_recv()
            target = lax.rem(place + k, 4)
            vsum[target] = vp[c, target] + vsib[target]
            for other in range(2):
                if k or other:
                    go(v_piece(k, other))

    def v_result():
        total = vsum[place, h]
        for k in range(4):
            for other in range(2):
                if k or other:
                    v_piece(k, other).wait_recv()
                    total = total + vrecv[k, other]
        out = unfold(total).T
        o_ref[0:96, :] = out[0:96, :]
        o_ref[96:192, :] = out[128:224, :]

    def spread_d():
        loads[1].wait()
        dsend[:, 0:96] = inp[1]
        dsend[:, 96:128] = jnp.zeros((192, 32), F32)
        go(d_copy)

    def turn_d():
        d_copy.wait_recv()
        for ref, plane in ((dsend, h), (drecv, 1 - h)):
            high, low = split(ref[...].T[0:96, :])
            dth[pl.ds(pl.multiple_of(plane * 96, 16), 96), :] = high
            dtl[pl.ds(pl.multiple_of(plane * 96, 16), 96), :] = low
        own_block(OLD_R)

    def load_m():
        loads[2].wait()
        pack(inp.at[2], pk.at[MOM])

    locals_of = dict(
        spread_d=spread_d, turn_d=turn_d, load_m=load_m, swap_start=swap_start, swap_end=swap_end,
        r_sibling=r_sibling, r_scatter=r_scatter, r_gather=r_gather, r_forward=r_forward,
        t_partial=t_partial, t_spread=t_spread, t_forward=t_forward, u_partial=u_partial,
        v_partial=v_partial, v_scatter=v_scatter, v_result=v_result,
    )
    d_copy = remote(dsend, drecv, d_s.at[0], d_r.at[0], partner)
    tmp[:, 96:128] = jnp.zeros((192, 32), F32)
    wide[...] = jnp.zeros((96, 256), F32)
    for _, name, m, s in sorted(EVENTS):
        if name == "ring":
            if s <= 8:
                send_step(m, s)
            if s == 1 and m != OLD_R:
                own_block(m)
            if s >= 2:
                take(m, s - 1)
        elif name == "fast":
            if s < 4:
                fast_step(s)
            if s >= 1:
                take(m, 2 * s - 1)
                take(m, 2 * s)
        else:
            action = locals_of[name]
            action(m) if m is not None else action()

    for copy in finish:
        copy.wait_send()

    @pl.when(half != h)
    def _():
        for m in (OLD_L, NEW_L):
            swap(m).wait_send()


def local(basis_new_left, basis_old_left, basis_new_right, basis_old_right, moment):
    vmem, dma = pltpu.VMEM, pltpu.SemaphoreType.DMA
    scratch = [
        vmem((5, 192, 96), F32), vmem((2, 144, 128), F32), vmem((96, 256), F32), vmem((192, 192), F32),
        vmem((4, 144, 128), F32), vmem((4, 2, 8, 144, 128), F32),
        vmem((192, 128), F32), vmem((192, 128), F32), vmem((192, 192), BF16), vmem((192, 192), BF16),
        vmem((192, 128), F32),
        vmem((2, 192, 768), F32), vmem((192, 768), F32), vmem((192, 768), F32),
        vmem((7, 24, 768), F32), vmem((2, 192, 768), F32),
        vmem((2, 192, 768), BF16), vmem((2, 192, 768), BF16),
        vmem((192, 2048), BF16), vmem((192, 2048), BF16), vmem((192, 2048), BF16), vmem((192, 2048), BF16),
        vmem((2, 144, 128), F32), vmem((144, 128), F32), vmem((144, 128), F32), vmem((2, 4, 2, 144, 128), F32),
        vmem((192, 2048), BF16), vmem((192, 2048), BF16),
        vmem((288, 128), F32), vmem((288, 128), F32),
        vmem((2, 4, 2, 144, 128), F32), vmem((4, 2, 144, 128), F32), vmem((4, 2, 144, 128), F32),
        vmem((4, 2, 144, 128), F32),
        dma((5,)), dma((2,)), dma((2,)), dma((4, 2, 8, NCH)), dma((4, 2, 8, NCH)), dma((1,)), dma((1,)),
        dma((2,)), dma((2,)), dma((2, 7)), dma((2, 7)), dma((2, 7)), dma((2, 7)), dma((2,)), dma((2,)),
        dma((1,)), dma((1,)), dma((4, 2)), dma((4, 2)), dma((1,)), dma((1,)), dma((1,)), dma((1,)),
        dma((4,)), dma((4,)), dma((4, 2)), dma((4, 2)),
    ]
    return pl.pallas_call(
        kernel,
        out_shape=jax.ShapeDtypeStruct((192, 96), F32),
        in_specs=[pl.BlockSpec(memory_space=pl.ANY)] * 5,
        out_specs=pl.BlockSpec(memory_space=pltpu.VMEM),
        scratch_shapes=scratch,
        compiler_params=pltpu.CompilerParams(
            collective_id=0, has_side_effects=True, vmem_limit_bytes=56 << 20
        ),
    )(basis_old_right, moment, basis_old_left, basis_new_left, basis_new_right)


def solution(mesh):
    placed = (P("row", "col"),) * 5
    return jax.shard_map(local, mesh=mesh, in_specs=placed, out_specs=P("row", "col"), check_vma=False)
```

time: 129 us -> 105 us (0.81); the launches traced: 127 us -> 105 us
  Pallas kernels: 122 us -> 103 us
  local copies, waits for them, and re-layouts: 5.1 us -> 1.54 us
    pallas_call x1, Pallas kernels: 122 us -> 103 us  [local(): pl.pallas_call(kernel, out_shape=jax.ShapeDtypeStruct((192, 96), F32), in...]
    unnamed x11 -> x1, local copies, waits for them, and re-layouts: 5.1 us -> 1.54 us
where the time goes in v2:
time: 105 us
  Pallas kernels  103 us (98%)
  local copies, waits for them, and re-layouts  1.54 us (1%)
    pallas_call x1, Pallas kernels, local(): pl.pallas_call(kernel, out_shape=jax.ShapeDtypeStruct((192, 96), F32), in...  103 us

profile of v2, /device:TPU:1, one launch (start us, length us, event | category | flops | bytes accessed | tf_op | source)
XLA Modules:
  0.0 104.5 jit_solution(17530193993242746207)
XLA Ops:
  0.0 103.0 %shard_map.55 = f32[192,96]{1,0:T(8,128)} custom-call(f32[192,96]{1,0:T(8,128)} %c_ref.1, f32[192,96]{1,0:T(8,128)} %m_ref.1, f32[192,96]{1,0:T(8,128)} %b_ref.1, f32[192,96]{1,0:T(8,128)} %a_ref.1, f32[192,96]{1,0:T(8,128)} %d_ref.1), custom_call_target="tpu_custom_call" | custom-call | tf_op jit(solution)/shard_map/pallas_call | solution.py:427
  103.0 1.5 %copy.7 = f32[192,96]{1,0:T(8,128)} copy(f32[192,96]{1,0:T(8,128)} %shard_map.55) | data formatting | bytes 147456

commit v3 on v2

v3 whole, which is shorter than its diff:
```python
import functools

import jax
import jax.numpy as jnp
from jax import lax
from jax.experimental import pallas as pl
from jax.experimental.pallas import tpu as pltpu
from jax.sharding import PartitionSpec as P

MESH = pl.DeviceIdType.MESH
F32, BF16 = jnp.float32, jnp.bfloat16
OLD_R, MOM, OLD_L, NEW_L = 0, 1, 2, 3
NCH = 2
FAST = (
    ((2, 1), (0,), ()), ((4, 3), (2, 1), ()), ((5,), (4, 3), (1, 2)), ((6,), (5,), (3, 4)),
    ((7,), (6,), (5,)), ((8,), (7,), (6,)), ((), (8,), (7, 8)),
)
ORDER = (
    "C0", "spread_d", "load_m", "M1", "swap_start:2", "swap_start:3", "turn_d",
    "C1", "M2", "C2", "M3", "swap_end:2", "swap_end:3",
    "C3", "r_scatter:0", "M4", "C4", "M5", "B1", "C5", "r_gather:0", "M6", "A1",
    "C6", "r_scatter:1", "M7", "B2", "A2",
    "r_gather:1", "t_first", "M8", "B3", "M9", "A3",
    "t_partial", "B4", "A4", "B5", "A5",
    "t_spread", "settle:70", "B6", "A6", "B7", "A7", "B8", "A8", "B9",
    "u_partial", "settle:20", "A9",
    "v_partial", "v_result",
)


def parsed(order):
    for token in order:
        name, _, value = token.partition(":")
        if name[0] in "CMBA":
            m = "CMBA".index(name[0])
            yield ("ring" if m else "fast"), m, int(name[1:])
        else:
            yield name, (int(value) if value else None), 0


NN = (((1,), (0,)), ((), ()))
NT = (((1,), (1,)), ((), ()))


def split(value):
    high = value.astype(BF16)
    return high, (value - high.astype(F32)).astype(BF16)


def dot3(a, b, dims):
    def one(u, v):
        return lax.dot_general(u, v, dims, preferred_element_type=F32)

    return one(a[0], b[0]) + (one(a[0], b[1]) + one(a[1], b[0]))


def kernel(c_ref, m_ref, b_ref, a_ref, d_ref, o_ref, *scratch):
    (inp, sw, wide, pk, pk2, rb, rb2, dd, dth, dtl, tmp, rp, rrs, rg, mh, ml, bh, bl, ah, al,
     tp, trecv, tfin, tg, th, tl, tsum, up, urecv, vp, vrecv,
     in_s, sw_s, sw_r, ring_s, ring_r, sh_s, sh_r, d_s, d_r, g3_s, g3_r, g5_s, g5_r,
     te_s, te_r, tm_s, tm_r, ue_s, ue_r, vr_s, vr_r) = scratch
    r, q = lax.axis_index("row"), lax.axis_index("col")
    p, c = r // 2, lax.rem(r, 2)
    h, z = q // 16, lax.rem(q, 16)
    half, place = p // 4, lax.rem(p, 4)
    sibling = (p * 2 + (1 - c), q)
    partner = (r, (1 - h) * 16 + z)
    ring_to = tuple((r, h * 16 + lax.rem(z + k, 16)) for k in (1, 15, 2, 14))

    def chip(k):
        return (lax.rem(p + k, 8) * 2 + c, q)

    def near(k, other, core=c):
        return ((4 * half + lax.rem(place + k, 4)) * 2 + core, ((1 - h) if other else h) * 16 + z)

    across = ((4 * (1 - half) + place) * 2 + c, (1 - h) * 16 + z)

    barrier = pltpu.get_barrier_semaphore()
    greeted = [sibling, across, *ring_to]
    greeted += [chip(k) for k in range(1, 8)] + [near(k, True) for k in range(4)]
    greeted += [near(k, other, 1 - c) for k in range(4) for other in range(2) if k or other]
    for device in greeted:
        pl.semaphore_signal(barrier, inc=1, device_id=device, device_id_type=MESH)

    loads = [pltpu.make_async_copy(ref, inp.at[i], in_s.at[i]) for i, ref in enumerate((c_ref, d_ref, m_ref, b_ref, a_ref))]
    for load in loads:
        load.start()

    def pack(source, dst):
        dst[:, 0:96] = source[0:144, :]
        for part in range(3):
            dst[48 * part:48 * part + 48, 96:128] = source[144:192, 32 * part:32 * part + 32]

    loads[0].wait()
    pack(inp.at[0], pk.at[OLD_R])
    tmp[:, 96:128] = jnp.zeros((192, 32), F32)
    wide[...] = jnp.zeros((96, 256), F32)
    pl.semaphore_wait(barrier, len(greeted))

    def remote(src, dst, send, recv, device):
        return pltpu.make_async_remote_copy(
            src_ref=src, dst_ref=dst, send_sem=send, recv_sem=recv, device_id=device, device_id_type=MESH
        )

    finish = []

    def settle(keep):
        while len(finish) > keep:
            finish.pop(0).wait_send()

    def go(copy):
        copy.start()
        finish.append(copy)
        return copy

    def ring(m, d, s, ch):
        if s == 8:
            rows, dst = pl.ds(72 * d, 72), rb.at[m, 0, 7]
        else:
            rows, dst = pl.ds(ch * (144 // NCH), 144 // NCH), rb.at[m, d, s - 1]
        back = 2 if m == OLD_R and s in (2, 4) else 1
        src = pk.at[m] if s == back else rb.at[m, d, s - back - 1]
        return remote(
            src.at[rows], dst.at[rows], ring_s.at[m, d, s - 1, ch], ring_r.at[m, d, s - 1, ch],
            ring_to[d + 2 * (back - 1)],
        )

    waited = set()

    def arrived(m, d, s, ch):
        if s >= 1 and (m, d, s, ch) not in waited:
            waited.add((m, d, s, ch))
            ring(m, d, s, ch).wait_recv()

    def send_step(m, s):
        for ch in range(NCH if s < 8 else 1):
            for d in range(2):
                for before in ([ch] if s < 8 else range(NCH)):
                    arrived(m, d, s - 1, before)
                go(ring(m, d, s, ch))

    def fast_step(s):
        sends, shares, takes = FAST[s]
        for offset in takes[:-1] if s == 6 else takes:
            take(OLD_R, offset)
        for ch in range(NCH):
            for offset in sends:
                if offset < 8 or ch == 0:
                    back = 2 if offset in (2, 4) else 1
                    for d in range(2):
                        if offset > back:
                            for before in ([ch] if offset < 8 else range(NCH)):
                                arrived(OLD_R, d, offset - back, before)
                        go(ring(OLD_R, d, offset, ch))
        for offset in shares:
            share(OLD_R, offset)
        if s == 6:
            take(OLD_R, takes[-1])

    def unpacked(src):
        lane = lax.broadcasted_iota(jnp.int32, (144, 128), 1)
        tmp[0:144, :] = jnp.where(lane < 96, src[...], 0.0)
        for part in range(3):
            tmp[144:192, 32 * part:32 * part + 32] = src[48 * part:48 * part + 48, 96:128]
        return split(tmp[...])

    def shared(m, d, s):
        src, dst = (pk.at[m], pk2.at[m]) if s == 0 else (rb.at[m, d, s - 1], rb2.at[m, d, s - 1])
        return remote(src, dst, sh_s.at[m, d, s], sh_r.at[m, d, s], sibling)

    def share(m, s):
        for d in range(2 if 0 < s < 8 else 1):
            if s > 0:
                for ch in range(NCH if s < 8 else 1):
                    arrived(m, d, s, ch)
            if s == 8:
                arrived(m, 1, 8, 0)
            go(shared(m, d, s))

    def store(m, d, e, own, other):
        one, two = unpacked(own), unpacked(other)
        high, low = (jnp.concatenate([u, v], axis=0) for u, v in zip(one, two))
        if m == OLD_R:
            rp[d, :, 96 * e:96 * e + 96] = dot3((dth[...], dtl[...]), (high, low), NN)[:, 0:96]
        elif m == MOM:
            mh[d, :, 96 * e:96 * e + 96] = high[:, 0:96]
            ml[d, :, 96 * e:96 * e + 96] = low[:, 0:96]
        else:
            origin = lax.rem(z + (16 - (e + 1) if d == 0 else e), 16)
            lanes = pl.ds(pl.multiple_of(origin * 128, 128), 128)
            hs, ls = (bh, bl) if m == OLD_L else (ah, al)
            hs[:, lanes] = high
            ls[:, lanes] = low

    def take(m, s):
        for d in range(2 if 0 < s < 8 else 1):
            shared(m, d, s).wait_recv()
        if s == 0:
            store(m, 1, 0, pk.at[m], pk2.at[m])
        else:
            store(m, 0, s - 1, rb.at[m, 0, s - 1], rb2.at[m, 0, s - 1])
            if s < 8:
                store(m, 1, s, rb.at[m, 1, s - 1], rb2.at[m, 1, s - 1])

    def swap(m):
        return remote(sw.at[m - 2], pk.at[m], sw_s.at[m - 2], sw_r.at[m - 2], across)

    def swap_start(m):
        loads[m + 1].wait()
        pack(inp.at[m + 1], sw.at[m - 2])

        @pl.when(half != h)
        def _():
            swap(m).start()

        @pl.when(half == h)
        def _():
            pltpu.make_async_copy(sw.at[m - 2], pk.at[m], sw_r.at[m - 2]).start()

    def swap_end(m):
        pltpu.make_async_copy(sw.at[m - 2], pk.at[m], sw_r.at[m - 2]).wait()
        share(m, 0)

    def r_piece(g, k):
        target = lax.rem(p + k, 8)
        rows = pl.ds(pl.multiple_of(target // 2 * 24, 8), 24)
        lanes = pl.ds(384 * g, 384)
        return remote(
            rp.at[lax.rem(target, 2), rows, lanes], rrs.at[k - 1, :, lanes], g3_s.at[g, k - 1], g3_r.at[g, k - 1], chip(k)
        )

    my_rows = pl.ds(pl.multiple_of(p // 2 * 24, 8), 24)

    def r_whole(g, k):
        mine = rg.at[lax.rem(p, 2), my_rows, pl.ds(384 * g, 384)]
        return remote(mine, mine, g5_s.at[g, k - 1], g5_r.at[g, k - 1], chip(k))

    def r_scatter(g):
        for k in range(1, 8):
            go(r_piece(g, k))

    def r_gather(g):
        lanes = pl.ds(384 * g, 384)
        total = rp[lax.rem(p, 2), my_rows, lanes]
        for k in range(1, 8):
            r_piece(g, k).wait_recv()
            total = total + rrs[k - 1, :, lanes]
        rg[lax.rem(p, 2), my_rows, lanes] = total
        for k in range(1, 8):
            go(r_whole(g, k))

    def t_half(g):
        for k in range(1, 8):
            r_whole(g, k).wait_recv()
        lanes = slice(384 * g, 384 * g + 384)
        total = None
        for d in range(2):
            term = dot3(split(rg[d, :, lanes]), (mh[d, :, lanes], ml[d, :, lanes]), NT)
            total = term if total is None else total + term
        return total

    def t_first():
        tsum[...] = t_half(0)

    def t_partial():
        total = tsum[...] + t_half(1)
        fold(tp.at[c], total[:, 0:96], total[:, 96:192])
        fold(tp.at[1 - c], total[:, 192:288], total[:, 288:384])
        go(t_exchange())

    def fold(dst, first, second):
        dst[0:96, 0:96] = first
        dst[0:96, 96:128] = second[:, 0:32]
        dst[96:144, 0:64] = second[0:48, 32:96]
        dst[96:144, 64:128] = second[48:96, 32:96]

    def unfold(value):
        wide[:, 0:96] = value[0:96, 0:96]
        wide[:, 128:160] = value[0:96, 96:128]
        wide[0:48, 160:224] = value[96:144, 0:64]
        wide[48:96, 160:224] = value[96:144, 64:128]
        return wide[...]

    def t_exchange():
        return remote(tp.at[1 - h], trecv, te_s.at[0], te_r.at[0], partner)

    def t_piece(k, other):
        return remote(tfin, tg.at[place, h], tm_s.at[k, other], tm_r.at[k, other], near(k, other))

    def t_spread():
        t_exchange().wait_recv()
        total = tp[h] + trecv[...]
        tfin[...] = total
        tg[place, h] = total
        for k in range(4):
            for other in range(2):
                if k or other:
                    go(t_piece(k, other))

    def u_exchange():
        return remote(up, urecv, ue_s.at[0], ue_r.at[0], chip(4))

    def u_partial():
        total = None
        for k in (0, 1, 3, 2):
            j = lax.rem(place + k, 4)
            for other in range(2):
                if k or other:
                    t_piece((4 - k) % 4, other).wait_recv()
            for core in range(2):
                lanes = slice(256 * core, 256 * core + 256)
                th[:, lanes], tl[:, lanes] = split(unfold(tg[j, core]))
            lanes = pl.ds(pl.multiple_of(512 * j, 512), 512)
            term = dot3((th[...], tl[...]), (bh[:, lanes], bl[:, lanes]), NT)
            total = term if total is None else total + term
        up[...] = total
        go(u_exchange())

    def v_piece(k, far):
        core = (1 - c) if far else c
        target = lax.rem(place + k, 4)
        device = ((4 * half + target) * 2 + core, c * 16 + z)
        return remote(vp.at[target, core], vrecv.at[k, h], vr_s.at[k, far], vr_r.at[k, h], device)

    def v_partial():
        u_exchange().wait_recv()
        whole = split(up[...] + urecv[...])
        for k in (1, 2, 3, 0):
            target = lax.rem(place + k, 4)
            for far in range(2):
                core = (1 - c) if far else c
                lanes = pl.ds(pl.multiple_of(256 * (2 * target + core), 256), 256)
                term = dot3(whole, (ah[:, lanes], al[:, lanes]), NN)
                fold(vp.at[target, core], term[:, 0:96], term[:, 128:224])
                if k or far:
                    go(v_piece(k, far))

        @pl.when(h != c)
        def _():
            v_piece(0, 0).start()

        @pl.when(h == c)
        def _():
            pltpu.make_async_copy(vp.at[place, c], vrecv.at[0, h], vr_r.at[0, h]).start()

    def v_result():
        total = None
        for k in range(4):
            for plane in range(2):
                pltpu.make_async_copy(vp.at[0, 0], vrecv.at[k, plane], vr_r.at[k, plane]).wait()
                total = vrecv[k, plane] if total is None else total + vrecv[k, plane]
        out = unfold(total).T
        o_ref[0:96, :] = out[0:96, :]
        o_ref[96:192, :] = out[128:224, :]

    row_of = lax.rem(c + h, 2)

    def d_near():
        return remote(inp.at[1], dd.at[row_of], d_s.at[0], d_r.at[row_of], sibling)

    def d_far():
        return remote(inp.at[1], dd.at[row_of], d_s.at[1], d_r.at[row_of], (p * 2 + h, (1 - h) * 16 + z))

    def spread_d():
        loads[1].wait()
        go(d_far())

        @pl.when(c != h)
        def _():
            d_near().start()

        @pl.when(c == h)
        def _():
            pltpu.make_async_copy(inp.at[1], dd.at[0], d_r.at[0]).start()

    def turn_d():
        for i in range(2):
            pltpu.make_async_copy(inp.at[1], dd.at[i], d_r.at[i]).wait()
            tmp[:, 0:96] = dd[i]
            dth[:, 192 * i:192 * i + 192], dtl[:, 192 * i:192 * i + 192] = split(tmp[...].T[0:96, :])
        take(OLD_R, 0)

    def load_m():
        loads[2].wait()
        pack(inp.at[2], pk.at[MOM])
        share(MOM, 0)

    locals_of = dict(
        spread_d=spread_d, turn_d=turn_d, load_m=load_m, swap_start=swap_start, swap_end=swap_end,
        r_scatter=r_scatter, r_gather=r_gather, t_first=t_first, t_partial=t_partial, t_spread=t_spread, u_partial=u_partial,
        v_partial=v_partial, v_result=v_result, settle=settle,
    )
    for name, m, s in parsed(ORDER):
        if name == "ring":
            if s >= 2:
                take(m, s - 2)
            if s <= 8:
                send_step(m, s)
            if s >= 2:
                share(m, s - 1)
            if s == 9:
                take(m, 8)
        elif name == "fast":
            fast_step(s)
        else:
            action = locals_of[name]
            action(m) if m is not None else action()

    settle(0)

    @pl.when(half != h)
    def _():
        for m in (OLD_L, NEW_L):
            swap(m).wait_send()

    @pl.when(c != h)
    def _():
        d_near().wait_send()
        v_piece(0, 0).wait_send()


def local(basis_new_left, basis_old_left, basis_new_right, basis_old_right, moment):
    vmem, dma = pltpu.VMEM, pltpu.SemaphoreType.DMA
    scratch = [
        vmem((5, 192, 96), F32), vmem((2, 144, 128), F32), vmem((96, 256), F32),
        vmem((4, 144, 128), F32), vmem((4, 144, 128), F32),
        vmem((4, 2, 8, 144, 128), F32), vmem((4, 2, 8, 144, 128), F32),
        vmem((2, 192, 96), F32), vmem((96, 384), BF16), vmem((96, 384), BF16), vmem((192, 128), F32),
        vmem((2, 96, 768), F32), vmem((7, 24, 768), F32), vmem((2, 96, 768), F32),
        vmem((2, 384, 768), BF16), vmem((2, 384, 768), BF16),
        vmem((384, 2048), BF16), vmem((384, 2048), BF16), vmem((384, 2048), BF16), vmem((384, 2048), BF16),
        vmem((2, 144, 128), F32), vmem((144, 128), F32), vmem((144, 128), F32), vmem((4, 2, 144, 128), F32),
        vmem((96, 512), BF16), vmem((96, 512), BF16), vmem((96, 384), F32), vmem((96, 384), F32), vmem((96, 384), F32),
        vmem((4, 2, 144, 128), F32), vmem((4, 2, 144, 128), F32),
        dma((5,)), dma((2,)), dma((2,)), dma((4, 2, 8, NCH)), dma((4, 2, 8, NCH)), dma((4, 2, 9)), dma((4, 2, 9)),
        dma((2,)), dma((2,)), dma((2, 7)), dma((2, 7)), dma((2, 7)), dma((2, 7)),
        dma((1,)), dma((1,)), dma((4, 2)), dma((4, 2)), dma((1,)), dma((1,)), dma((4, 2)), dma((4, 2)),
    ]
    return pl.pallas_call(
        kernel,
        out_shape=jax.ShapeDtypeStruct((192, 96), F32),
        in_specs=[pl.BlockSpec(memory_space=pl.ANY)] * 5,
        out_specs=pl.BlockSpec(memory_space=pltpu.VMEM),
        scratch_shapes=scratch,
        compiler_params=pltpu.CompilerParams(
            collective_id=0, has_side_effects=True, vmem_limit_bytes=56 << 20
        ),
    )(basis_old_right, moment, basis_old_left, basis_new_left, basis_new_right)


def solution(mesh):
    placed = (P("row", "col"),) * 5
    return jax.shard_map(local, mesh=mesh, in_specs=placed, out_specs=P("row", "col"), check_vma=False)
```

time: 105 us -> 102 us (0.971)
  Pallas kernels: 103 us -> 101 us
    pallas_call x1, Pallas kernels: 103 us -> 101 us  [local(): pl.pallas_call(kernel, out_shape=jax.ShapeDtypeStruct((192, 96), F32), in...]
where the time goes in v3:
time: 102 us
  Pallas kernels  101 us (99%)
  local copies, waits for them, and re-layouts  1.54 us (2%)
    pallas_call x1, Pallas kernels, local(): pl.pallas_call(kernel, out_shape=jax.ShapeDtypeStruct((192, 96), F32), in...  101 us

profile of v3, /device:TPU:1, one launch (start us, length us, event | category | flops | bytes accessed | tf_op | source)
XLA Modules:
  0.0 102.1 jit_solution(14392964604772233701)
XLA Ops:
  0.0 100.5 %shard_map.55 = f32[192,96]{1,0:T(8,128)} custom-call(f32[192,96]{1,0:T(8,128)} %c_ref.1, f32[192,96]{1,0:T(8,128)} %m_ref.1, f32[192,96]{1,0:T(8,128)} %b_ref.1, f32[192,96]{1,0:T(8,128)} %a_ref.1, f32[192,96]{1,0:T(8,128)} %d_ref.1), custom_call_target="tpu_custom_call" | custom-call | tf_op jit(solution)/shard_map/pallas_call | solution.py:439
  100.6 1.5 %copy.7 = f32[192,96]{1,0:T(8,128)} copy(f32[192,96]{1,0:T(8,128)} %shard_map.55) | data formatting | bytes 147456

commit v4 on v3

--- a/solution.py
+++ b/solution.py
@@ -75,16 +75,16 @@
 
     across = ((4 * (1 - half) + place) * 2 + c, (1 - h) * 16 + z)
 
-    barrier = pltpu.get_barrier_semaphore()
-    greeted = [sibling, across, *ring_to]
-    greeted += [chip(k) for k in range(1, 8)] + [near(k, True) for k in range(4)]
-    greeted += [near(k, other, 1 - c) for k in range(4) for other in range(2) if k or other]
-    for device in greeted:
-        pl.semaphore_signal(barrier, inc=1, device_id=device, device_id_type=MESH)
-
     loads = [pltpu.make_async_copy(ref, inp.at[i], in_s.at[i]) for i, ref in enumerate((c_ref, d_ref, m_ref, b_ref, a_ref))]
     for load in loads:
         load.start()
+
+    barrier = pltpu.get_barrier_semaphore()
+    greeted = [across]
+    greeted += [near(k, other, 1 - c) for k in range(4) for other in range(2) if k or other]
+    greeted += [near(k, True) for k in range(4)] + [chip(k) for k in range(1, 8)] + [*ring_to, sibling]
+    for device in greeted:
+        pl.semaphore_signal(barrier, inc=1, device_id=device, device_id_type=MESH)
 
     def pack(source, dst):
         dst[:, 0:96] = source[0:144, :]

time: 102 us -> 102 us (level)
  no operation moved by 1% of the time
where the time goes in v4:
time: 102 us
  Pallas kernels  101 us (99%)
  local copies, waits for them, and re-layouts  1.54 us (2%)
    pallas_call x1, Pallas kernels, local(): pl.pallas_call(kernel, out_shape=jax.ShapeDtypeStruct((192, 96), F32), in...  101 us

profile of v4, /device:TPU:1, one launch (start us, length us, event | category | flops | bytes accessed | tf_op | source)
XLA Modules:
  0.0 102.1 jit_solution(3827305440125245420)
XLA Ops:
  0.0 100.5 %shard_map.55 = f32[192,96]{1,0:T(8,128)} custom-call(f32[192,96]{1,0:T(8,128)} %c_ref.1, f32[192,96]{1,0:T(8,128)} %m_ref.1, f32[192,96]{1,0:T(8,128)} %b_ref.1, f32[192,96]{1,0:T(8,128)} %a_ref.1, f32[192,96]{1,0:T(8,128)} %d_ref.1), custom_call_target="tpu_custom_call" | custom-call | tf_op jit(solution)/shard_map/pallas_call | solution.py:439
  100.6 1.5 %copy.7 = f32[192,96]{1,0:T(8,128)} copy(f32[192,96]{1,0:T(8,128)} %shard_map.55) | data formatting | bytes 147456
